TPU v7x, 32 devices: a whole 2x2x4 slice. The times are simulated.
32 devices in a mesh: blk: 4 (over y, x), group: 8 (over z, core).
Axes of the slice: x: 2, y: 2, z: 4, core: 2. Of those that a mesh axis runs over, the one named last changes fastest.
Arguments:
- star_pos: float32 [3, 32768], P(None, 'blk'), may hold values from -6 to 6
- star_vel: float32 [3, 32768], P(None, 'blk'), may hold values from -6 to 6
- star_acc: float32 [3, 32768], P(None, 'blk'), may hold values from -6 to 6
- star_jerk: float32 [3, 32768], P(None, 'blk'), may hold values from -6 to 6
- star_mass: float32 [32768], P('blk'), may hold values from 0.25 to 4
- star_dt: float32 [32768], P('blk'), may hold values from 0.0625 to 1
- active_list: int32 [4, 8, 128], P('blk', 'group'), may hold values from 0 to 8191
- active_count: int32 [4, 8], P('blk', 'group'), may hold values from 1 to 128, 256 in all within a row
Outputs:
- accel_jerk: float32 [4, 8, 6, 128], P('blk', 'group')
Inputs may be any that keep to these rules, and one draw needn't show every extreme that they name: `active_list`: only the first active_count slots of a list are active, the rest are ignored; entries may repeat. `active_count`: for each blk index the counts over group sum to 256, and one of them is exactly 128.
All inputs are finite; a program needn't handle non-finite values.
Results may differ from a plain program's by a relative error of at most 0.00012.
Values sent between devices are 32-bit elements; how exact they have to be, the bound alone decides.
No kernel may reach another device: no remote copies, remote signals or barrier semaphores. Data moves between devices by JAX's collectives and lax.ppermute only.
A program may use at most 64 MiB of HBM per device.

v0:
```python
import functools

import jax
import jax.numpy as jnp
from jax import lax
from jax.experimental import pallas as pl
from jax.experimental.pallas import tpu as pltpu
from jax.sharding import PartitionSpec as P

LANES = 128
LANE_BITS = 7
SOFTEN = 0.01
VMEM_LIMIT = 48 * 1024 * 1024
SPREAD = 32
SHARERS = 4
SENT = 7
LEAN = 4


def predict_chunk(pos, vel, acc, jerk, mass, delta, chunk, total_stars):
    lanes = pl.ds(pl.multiple_of(chunk * LANES, LANES), LANES)
    step = delta[pl.ds(chunk, 1), :]
    p, v, a, j = pos[:, lanes], vel[:, lanes], acc[:, lanes], jerk[:, lanes]
    ppos = p + step * (v + step * (0.5 * a + step * (j / 6.0)))
    pvel = v + step * (a + step * (0.5 * j))
    weight = mass[pl.ds(chunk, 1), :] / total_stars
    return jnp.concatenate([ppos, pvel, weight, weight], 0)


def predict_kernel(total_stars, *refs):
    raw, count, (full, part, half, packed) = refs[:7], refs[7], refs[8:12]
    held, sems = refs[12:19], refs[19]
    copies = [
        pltpu.make_async_copy(source, target, sems.at[i])
        for i, (source, target) in enumerate(zip(raw, held))
    ]
    for copy in copies:
        copy.start()
    for copy in copies:
        copy.wait()

    def one(c, _):
        state = predict_chunk(*held[:6], c, total_stars)
        full[pl.ds(pl.multiple_of(c * 8, 8), 8), :] = state
        return _

    lax.fori_loop(0, full.shape[0] // 8, one, 0, unroll=8)
    for out in (part, half):
        size = out.shape[0] // SENT
        base = lax.rem(lax.axis_index("group"), full.shape[0] // (8 * size)) * size
        for c in range(size):
            state = full[pl.ds(pl.multiple_of((base + c) * 8, 8), 8), :]
            out[c * SENT : (c + 1) * SENT, :] = state[:SENT]
    packed[...] = jnp.zeros_like(packed)
    packed[0:1, :] = held[6][...]
    packed[1:2, :] = jnp.full((1, LANES), count[0, 0], jnp.int32)


def pair_terms(rows, stars, base, total):
    star = [stars[pl.ds(base + i, 1), :] for i in range(7)]
    dx, dy, dz, ux, uy, uz = (star[i] - rows[i] for i in range(6))
    inverse = lax.rsqrt(dx * dx + dy * dy + dz * dz + SOFTEN)
    square = inverse * inverse
    cube = (star[6] * inverse) * square
    radial = (dx * ux + dy * uy + dz * uz) * square
    ax, ay, az = dx * cube, dy * cube, dz * cube
    terms = (ax, ay, az, ux * cube, uy * cube, uz * cube, radial * ax, radial * ay, radial * az)
    return tuple(t + x for t, x in zip(total, terms))


def gather(lists, full, splat):
    slots = lists.shape[1]
    width = SHARERS * slots
    lane = lax.broadcasted_iota(jnp.int32, (8, width), 1)
    whole, base = None, 0
    for i in range(SHARERS):
        index = jnp.broadcast_to(lists[2 * i : 2 * i + 1, :], (8, slots))
        wide = jnp.concatenate([index] * SHARERS, 1)
        whole = jnp.where(lane >= base, pltpu.roll(wide, base, 1), whole) if i else wide
        base = base + lists[2 * i + 1, 0]
    for block in range(SHARERS):

        @pl.when(base > block * slots)
        def _():
            index = whole[:, block * slots : (block + 1) * slots]
            place = index & (LANES - 1)
            chunk = lax.shift_right_logical(index, LANE_BITS)

            def look(c, found):
                state = full[pl.ds(pl.multiple_of(c * 8, 8), 8), :]
                here = jnp.take_along_axis(state, place, axis=1, mode="promise_in_bounds")
                return jnp.where(chunk == c, here, found)

            found = lax.fori_loop(
                0, full.shape[0] // 8, look, jnp.zeros((8, slots), jnp.float32), unroll=16
            )
            for piece in range(0, slots, SPREAD):

                @pl.when(base > block * slots + piece)
                def _():
                    for row in range(piece, piece + SPREAD):
                        first = (block * slots + row) * 8
                        splat[first : first + 8, :] = jnp.broadcast_to(
                            found[:, row : row + 1], (8, LANES)
                        )


def group_bounds(lists):
    counts = [lists[2 * owner + 1, 0] for owner in range(SHARERS)]
    there, here = counts[0] + counts[1], counts[2] + counts[3]
    return (jnp.maximum(there, here) + 7) // 8, (there + here + 7) // 8


def add_lanes(begin, end, sums, flat):
    slots = flat.shape[1] // SHARERS
    for block in range(SHARERS):

        @pl.when((end * 8 > block * slots) & (begin * 8 < (block + 1) * slots))
        def _():
            part = pl.ds(block * slots, slots)
            for j in range(6):
                flat[pl.ds(j, 1), part] = jnp.sum(sums[j, part, :], axis=1)[None, :]


def cut(lists, owner, flat, slots):
    first = sum(lists[2 * before + 1, 0] for before in range(owner))
    return pltpu.roll(flat, flat.shape[1] - first, 1)[:, :slots] if owner else flat[:, :slots]


def add_forces(begin, end, splat, stars, chunks, stride, unroll, before, after, height=8):
    def group(g, _):
        place = pl.multiple_of(g * height, 8)
        rows = [
            jnp.concatenate(
                [splat[pl.ds((place + k) * 8 + i, 8, stride=8), :] for k in range(0, height, 8)], 0
            )
            for i in range(6)
        ]
        zero = jnp.zeros((height, LANES), jnp.float32)
        if before is None:
            total = (zero,) * 9
        else:
            total = tuple(before[i, pl.ds(place, height), :] for i in range(6)) + (zero,) * 3
        total = lax.fori_loop(
            0,
            chunks[1],
            lambda c, t: pair_terms(rows, stars, (chunks[0] + c) * stride, t),
            total,
            unroll=unroll,
        )
        for i in range(3):
            after[i, pl.ds(place, height), :] = total[i]
            after[3 + i, pl.ds(place, height), :] = total[3 + i] - 3.0 * total[6 + i]
        return _

    lax.fori_loop(begin, end, group, 0)


def near_kernel(lists, full, splat, sums):
    gather(lists, full, splat)
    _, groups = group_bounds(lists)
    size = full.shape[0] // (8 * SHARERS)
    place = lax.rem(lax.axis_index("group"), SHARERS)
    odd = lax.rem(place, 2)
    groups = (groups + 1) // 2
    first, less, more = place * size - odd * LEAN, size - LEAN, 2 * LEAN
    add_forces(0, groups, splat, full, (first, less), 8, less, None, sums, 16)
    add_forces(0, groups * odd, splat, full, (first + less, more), 8, more, sums, sums, 16)


def there_kernel(*refs):
    lists, splat, sums = refs[:3]
    parts, (blocks, flat, stars, held) = refs[3:-4], refs[-4:]
    begin = 0
    for part in parts:
        stars[pl.ds(begin, part.shape[0]), :] = part[...]
        begin += part.shape[0]
    shared, _ = group_bounds(lists)
    far = (0, stars.shape[0] // SENT)
    add_forces(0, shared, splat, stars, far, SENT, 48, sums, held)
    add_lanes(0, shared, held, flat)
    for owner in range(2):
        blocks[owner * 8 : owner * 8 + 8, :] = cut(lists, owner, flat[...], blocks.shape[1])


def here_kernel(lists, splat, sums, stars, flat, mine, other, held, rest):
    shared, groups = group_bounds(lists)
    far = (0, stars.shape[0] // SENT)
    add_forces(shared, groups, splat, stars, far, SENT, 48, sums, held)
    add_lanes(shared, groups, held, rest)
    done = lax.broadcasted_iota(jnp.int32, flat.shape, 1) < shared * 8
    whole = jnp.where(done, flat[...], rest[...])
    for owner, out in ((2, mine), (3, other)):
        out[...] = cut(lists, owner, whole, out.shape[1])


def on_device(
    star_pos, star_vel, star_acc, star_jerk, star_mass, star_dt, active_list, active_count
):
    n_blk = lax.axis_size("blk")
    n_group = lax.axis_size("group")
    shard = star_mass.shape[0]
    total_stars = shard * n_blk
    slots = active_list.shape[2]
    chunks = shard // LANES
    room = SHARERS * slots
    vmem = pl.BlockSpec(memory_space=pltpu.VMEM)
    smem = pl.BlockSpec(memory_space=pltpu.SMEM)
    params = pltpu.CompilerParams(vmem_limit_bytes=VMEM_LIMIT)
    splat_type = jax.ShapeDtypeStruct((room * 8, LANES), jnp.float32)
    sums_type = jax.ShapeDtypeStruct((6, room, LANES), jnp.float32)
    raw = (
        star_pos,
        star_vel,
        star_acc,
        star_jerk,
        star_mass.reshape(chunks, LANES),
        star_dt.reshape(chunks, LANES),
        active_list[0],
    )

    def swap(x, axis, bits):
        return lax.ppermute(x, axis, [(i, i ^ bits) for i in range(lax.axis_size(axis))])

    def trade(x, step):
        pairs = [
            (b * n_group + g, (b ^ step ^ (2 if g & 2 else 1)) * n_group + g)
            for b in range(n_blk)
            for g in range(n_group)
        ]
        return lax.ppermute(x, ("blk", "group"), pairs)

    part_type = jax.ShapeDtypeStruct((chunks * SENT // SHARERS, LANES), jnp.float32)
    full, part, half, packed = pl.pallas_call(
        functools.partial(predict_kernel, total_stars),
        out_shape=(
            jax.ShapeDtypeStruct((chunks * 8, LANES), jnp.float32),
            part_type,
            jax.ShapeDtypeStruct((chunks * SENT // 2, LANES), jnp.float32),
            jax.ShapeDtypeStruct((8, slots), jnp.int32),
        ),
        in_specs=[pl.BlockSpec(memory_space=pltpu.HBM)] * 7 + [smem],
        out_specs=(vmem,) * 4,
        scratch_shapes=[pltpu.VMEM(x.shape, x.dtype) for x in raw]
        + [pltpu.SemaphoreType.DMA((7,))],
        compiler_params=params,
        name="predict",
    )(*(pltpu.with_memory_space_constraint(x, pltpu.HBM) for x in raw), active_count)
    parts = []
    for step in range(0, n_blk, 4):
        parts.append(trade(half, step))
        parts += [swap(part, "blk", bits) for bits in (step + 3, step) if bits]
    core, *others = (swap(packed, "group", bits) for bits in range(1, SHARERS))
    lists = jnp.concatenate([x[:2] for x in (*others, packed, core)], 0)
    splat, sums = pl.pallas_call(
        near_kernel,
        out_shape=(splat_type, sums_type),
        in_specs=[vmem] * 2,
        out_specs=(vmem,) * 2,
        compiler_params=params,
        name="near_forces",
    )(lists, full)
    block_type = jax.ShapeDtypeStruct((8, slots), jnp.float32)
    pairs = slots * shard
    cost = pl.CostEstimate(flops=40 * pairs, bytes_accessed=pairs, transcendentals=pairs)
    flat_type = jax.ShapeDtypeStruct((8, SHARERS * slots), jnp.float32)
    stars_type = jax.ShapeDtypeStruct((sum(x.shape[0] for x in parts), LANES), jnp.float32)
    there, flat, stars = pl.pallas_call(
        there_kernel,
        out_shape=(
            jax.ShapeDtypeStruct((16, slots), jnp.float32),
            flat_type,
            stars_type,
        ),
        in_specs=[vmem] * (3 + len(parts)),
        out_specs=(vmem,) * 3,
        scratch_shapes=[pltpu.VMEM(sums_type.shape, jnp.float32)],
        compiler_params=params,
        cost_estimate=cost,
        name="there_forces",
    )(lists, splat, sums, *parts)
    returned = swap(there, "group", 2)
    mine, other = pl.pallas_call(
        here_kernel,
        out_shape=(block_type, block_type),
        in_specs=[vmem] * 5,
        out_specs=(vmem,) * 2,
        scratch_shapes=[
            pltpu.VMEM(sums_type.shape, jnp.float32),
            pltpu.VMEM(flat_type.shape, jnp.float32),
        ],
        compiler_params=params,
        cost_estimate=cost,
        name="here_forces",
    )(lists, splat, sums, stars, flat)
    total = mine + returned[:8] + swap(other + returned[8:], "group", 1)
    live = lax.broadcasted_iota(jnp.int32, (1, slots), 1) < packed[1:2]
    output = jnp.where(live, total[:6], 0.0)
    return output[None, None]


def solution(mesh):
    return jax.shard_map(
        on_device,
        mesh=mesh,
        in_specs=(
            P(None, "blk"),
            P(None, "blk"),
            P(None, "blk"),
            P(None, "blk"),
            P("blk"),
            P("blk"),
            P("blk", "group", None),
            P("blk", "group"),
        ),
        out_specs=P("blk", "group", None, None),
        check_vma=False,
    )
```

profile of v0, /device:TPU:23, one launch (start us, length us, event | category | flops | bytes accessed | tf_op | source)
XLA Modules:
  0.0 23.5 jit_solution(5129511350104419872)
XLA Ops:
  0.7 1.4 %predict.1 = (f32[512,128]{1,0:T(8,128)S(1)}, f32[112,128]{1,0:T(8,128)S(1)}, f32[224,128]{1,0:T(8,128)S(1)}, s32[8,128]{1,0:T(8,128)S(1)}) custom-call(f32[3,8192]{1,0:T(4,128)} %refs_0_.1, f32[3,8192]{1,0:T(4,128)} %refs_1_.1, f32[3,8192]{1,0:T(4,128)} %refs_2_.1, f32[3,8192]{1,0:T(4,128)} %refs_3_.1, f32[64,128]{1,0:T(8,128)} %bitcast.7, ...), custom_call_target="tpu_custom_call" | custom-call | tf_op jit(solution)/shard_map/predict/pallas_call | solution.py:234
  2.1 0.7 %collective-permute-start.2 = (s32[8,128]{1,0:T(8,128)S(1)}, s32[8,128]{1,0:T(8,128)S(1)}, u32[]{:S(2)}, u32[]{:S(2)}) collective-permute-start(s32[8,128]{1,0:T(8,128)S(1)} %get-tuple-element.16), channel_id=1, source_target_pairs={{0,1},{1,0},{2,3},{3,2},{4,5},{5,4},{6,7},{7,6},{8,9},{9,8},{10,11... | collective-permute-start | bytes 12296 | tf_op jit(solution)/shard_map/ppermute | solution.py:223
  2.8 1.3 %collective-permute-start.1 = (s32[8,128]{1,0:T(8,128)S(1)}, s32[8,128]{1,0:T(8,128)S(1)}, u32[]{:S(2)}, u32[]{:S(2)}) collective-permute-start(s32[8,128]{1,0:T(8,128)S(1)} %get-tuple-element.16), channel_id=1, source_target_pairs={{0,3},{1,2},{2,1},{3,0},{4,7},{5,6},{6,5},{7,4},{8,11},{9,10},{10,... | collective-permute-start | bytes 12296 | tf_op jit(solution)/shard_map/ppermute | solution.py:223
  4.1 0.2 collective-permute-start
  4.2 0.3 %collective-permute-start.3 = (f32[224,128]{1,0:T(8,128)S(1)}, f32[224,128]{1,0:T(8,128)S(1)}, u32[]{:S(2)}, u32[]{:S(2)}) collective-permute-start(f32[224,128]{1,0:T(8,128)S(1)} %get-tuple-element.20), channel_id=1, source_target_pairs={{0,8},{1,9},{2,18},{3,19},{4,12},{5,13},{6,22},{7,23},{8,0},{9,1},... | collective-permute-start | bytes 344072 | tf_op jit(solution)/shard_map/ppermute | solution.py:231
  4.5 1.2 %collective-permute-start.4 = (f32[112,128]{1,0:T(8,128)S(1)}, f32[112,128]{1,0:T(8,128)S(1)}, u32[]{:S(2)}, u32[]{:S(2)}) collective-permute-start(f32[112,128]{1,0:T(8,128)S(1)} %get-tuple-element.21), channel_id=1, source_target_pairs={{0,24},{8,16},{16,8},{24,0},{1,25},{9,17},{17,9},{25,1},{2,26},{10... | collective-permute-start | bytes 172040 | tf_op jit(solution)/shard_map/ppermute | solution.py:223
  5.7 0.0 collective-permute-done.2
  5.7 0.2 collective-permute-done.1
  5.9 0.7 %collective-permute-done = s32[8,128]{1,0:T(8,128)S(1)} collective-permute-done((s32[8,128]{1,0:T(8,128)S(1)}, s32[8,128]{1,0:T(8,128)S(1)}, u32[]{:S(2)}, u32[]{:S(2)}) %collective-permute-start) | collective-permute-done | bytes 4128 | tf_op jit(solution)/shard_map/ppermute | solution.py:223
  6.6 5.0 %near_forces.1 = (f32[4096,128]{1,0:T(8,128)S(1)}, f32[6,512,128]{2,1,0:T(8,128)S(1)}) custom-call(s32[8,128]{1,0:T(8,128)S(1)} %pad_add_fusion.lists.refs_0_, f32[512,128]{1,0:T(8,128)S(1)} %get-tuple-element.17.full), custom_call_target="tpu_custom_call" | custom-call | tf_op jit(solution)/shard_map/near_forces/pallas_call | solution.py:255
  11.6 0.0 collective-permute-done.4.refs_4_
  11.6 0.0 collective-permute-done.3.refs_3_
  11.6 6.6 %there_forces.1 = (f32[16,128]{1,0:T(8,128)S(1)}, f32[8,512]{1,0:T(8,128)S(1)}, f32[336,128]{1,0:T(8,128)S(1)}) custom-call(s32[8,128]{1,0:T(8,128)S(1)} %pad_add_fusion.lists.refs_0_, f32[4096,128]{1,0:T(8,128)S(1)} %get-tuple-element.18.refs_1_.splat, f32[6,512,128]{2,1,0:T(8,128)S(1)} %get-tuple-element.19.refs_2_.sums, ...), custom_call_target="tpu_custom_call" | custom-call | flops 41943040 | bytes 1048576 | tf_op jit(solution)/shard_map/there_forces/pallas_call | solution.py:268
  18.2 0.7 %collective-permute-start.5 = (f32[16,128]{1,0:T(8,128)S(1)}, f32[16,128]{1,0:T(8,128)S(1)}, u32[]{:S(2)}, u32[]{:S(2)}) collective-permute-start(f32[16,128]{1,0:T(8,128)S(1)} %get-tuple-element.25), channel_id=1, source_target_pairs={{0,2},{1,3},{2,0},{3,1},{4,6},{5,7},{6,4},{7,5},{8,10},{9,11},{10,... | collective-permute-start | bytes 24584 | tf_op jit(solution)/shard_map/ppermute | solution.py:223
  18.9 1.7 %here_forces.1 = (f32[8,128]{1,0:T(8,128)S(1)}, f32[8,128]{1,0:T(8,128)S(1)}) custom-call(s32[8,128]{1,0:T(8,128)S(1)} %pad_add_fusion.lists.refs_0_, f32[4096,128]{1,0:T(8,128)S(1)} %get-tuple-element.18.refs_1_.splat, f32[6,512,128]{2,1,0:T(8,128)S(1)} %get-tuple-element.19.refs_2_.sums, f32[336,128]{1,0:T(8,128)S(1)} %get-tuple-element.22.stars, ...), custom_call_target="tpu_custom_call" | custom-call | flops 41943040 | bytes 1048576 | tf_op jit(solution)/shard_map/here_forces/pallas_call | solution.py:283
  20.6 0.1 collective-permute-done.5
  20.7 1.3 %collective-permute-start.6 = (f32[8,128]{1,0:T(8,128)S(1)}, f32[8,128]{1,0:T(8,128)S(1)}, u32[]{:S(2)}, u32[]{:S(2)}) collective-permute-start(f32[8,128]{1,0:T(8,128)S(1)} %slice_add_fusion), channel_id=1, source_target_pairs={{0,1},{1,0},{2,3},{3,2},{4,5},{5,4},{6,7},{7,6},{8,9},{9,8},{10,11... | collective-permute-start | bytes 12296 | tf_op jit(solution)/shard_map/ppermute | solution.py:223
  22.1 0.8 %collective-permute-done.6 = f32[8,128]{1,0:T(8,128)S(1)} collective-permute-done((f32[8,128]{1,0:T(8,128)S(1)}, f32[8,128]{1,0:T(8,128)S(1)}, u32[]{:S(2)}, u32[]{:S(2)}) %collective-permute-start.6) | collective-permute-done | bytes 4128 | tf_op jit(solution)/shard_map/ppermute | solution.py:223
  22.9 0.6 %copy.9 = f32[1,1,6,128]{3,1,2,0:T(1,128)} copy(f32[1,1,6,128]{3,2,1,0:T(8,128)S(1)} %select_bitcast_fusion) | data formatting | bytes 6144 | tf_op jit(solution)/shard_map/broadcast_in_dim | solution.py:299
  (9 shorter events, 0.0 us)
Async XLA Ops:
  2.1 3.6 %collective-permute-start.2 = (s32[8,128]{1,0:T(8,128)S(1)}, s32[8,128]{1,0:T(8,128)S(1)}, u32[]{:S(2)}, u32[]{:S(2)}) collective-permute-start(s32[8,128]{1,0:T(8,128)S(1)} %get-tuple-element.16), channel_id=1, source_target_pairs={{0,1},{1,0},{2,3},{3,2},{4,5},{5,4},{6,7},{7,6},{8,9},{9,8},{10,11... | collective-permute-start | bytes 12296 | tf_op jit(solution)/shard_map/ppermute | solution.py:223
  2.8 3.0 %collective-permute-start.1 = (s32[8,128]{1,0:T(8,128)S(1)}, s32[8,128]{1,0:T(8,128)S(1)}, u32[]{:S(2)}, u32[]{:S(2)}) collective-permute-start(s32[8,128]{1,0:T(8,128)S(1)} %get-tuple-element.16), channel_id=1, source_target_pairs={{0,3},{1,2},{2,1},{3,0},{4,7},{5,6},{6,5},{7,4},{8,11},{9,10},{10,... | collective-permute-start | bytes 12296 | tf_op jit(solution)/shard_map/ppermute | solution.py:223
  4.1 2.5 %collective-permute-start = (s32[8,128]{1,0:T(8,128)S(1)}, s32[8,128]{1,0:T(8,128)S(1)}, u32[]{:S(2)}, u32[]{:S(2)}) collective-permute-start(s32[8,128]{1,0:T(8,128)S(1)} %get-tuple-element.16), channel_id=1, source_target_pairs={{0,2},{1,3},{2,0},{3,1},{4,6},{5,7},{6,4},{7,5},{8,10},{9,11},{10,... | collective-permute-start | bytes 12296 | tf_op jit(solution)/shard_map/ppermute | solution.py:223
  4.2 7.3 %collective-permute-start.3 = (f32[224,128]{1,0:T(8,128)S(1)}, f32[224,128]{1,0:T(8,128)S(1)}, u32[]{:S(2)}, u32[]{:S(2)}) collective-permute-start(f32[224,128]{1,0:T(8,128)S(1)} %get-tuple-element.20), channel_id=1, source_target_pairs={{0,8},{1,9},{2,18},{3,19},{4,12},{5,13},{6,22},{7,23},{8,0},{9,1},... | collective-permute-start | bytes 344072 | tf_op jit(solution)/shard_map/ppermute | solution.py:231
  4.5 7.1 %collective-permute-start.4 = (f32[112,128]{1,0:T(8,128)S(1)}, f32[112,128]{1,0:T(8,128)S(1)}, u32[]{:S(2)}, u32[]{:S(2)}) collective-permute-start(f32[112,128]{1,0:T(8,128)S(1)} %get-tuple-element.21), channel_id=1, source_target_pairs={{0,24},{8,16},{16,8},{24,0},{1,25},{9,17},{17,9},{25,1},{2,26},{10... | collective-permute-start | bytes 172040 | tf_op jit(solution)/shard_map/ppermute | solution.py:223
  18.2 2.5 %collective-permute-start.5 = (f32[16,128]{1,0:T(8,128)S(1)}, f32[16,128]{1,0:T(8,128)S(1)}, u32[]{:S(2)}, u32[]{:S(2)}) collective-permute-start(f32[16,128]{1,0:T(8,128)S(1)} %get-tuple-element.25), channel_id=1, source_target_pairs={{0,2},{1,3},{2,0},{3,1},{4,6},{5,7},{6,4},{7,5},{8,10},{9,11},{10,... | collective-permute-start | bytes 24584 | tf_op jit(solution)/shard_map/ppermute | solution.py:223
  20.7 2.2 %collective-permute-start.6 = (f32[8,128]{1,0:T(8,128)S(1)}, f32[8,128]{1,0:T(8,128)S(1)}, u32[]{:S(2)}, u32[]{:S(2)}) collective-permute-start(f32[8,128]{1,0:T(8,128)S(1)} %slice_add_fusion), channel_id=1, source_target_pairs={{0,1},{1,0},{2,3},{3,2},{4,5},{5,4},{6,7},{7,6},{8,9},{9,8},{10,11... | collective-permute-start | bytes 12296 | tf_op jit(solution)/shard_map/ppermute | solution.py:223
where the time goes:
time: 23.7 us; the launch traced here: 23.5 us
  Pallas kernels  14.8 us (62%)
  starting transfers between devices  5.58 us (24%)
  waiting for transfers between devices  1.82 us (8%)
  between operations  0.69 us (3%)
  local copies, waits for them, and re-layouts  0.59 us (2%)
    pallas_call x1, Pallas kernels, on_device(): pl.pallas_call(there_kernel, out_shape=(jax.ShapeDtypeStruct((16, slots),...  6.62 us
    ppermute x6, starting transfers between devices, swap(): lax.ppermute(x, axis, [(i, i ^ bits) for i in range(lax.axis_size(axis))])  5.32 us
    pallas_call x1, Pallas kernels, on_device(): pl.pallas_call(near_kernel, out_shape=(splat_type, sums_type), in_specs=[...  5.03 us
    ppermute x6, waiting for transfers between devices, swap(): lax.ppermute(x, axis, [(i, i ^ bits) for i in range(lax.axis_size(axis))])  1.81 us
    pallas_call x1, Pallas kernels, on_device(): pl.pallas_call(here_kernel, out_shape=(block_type, block_type), in_specs=...  1.73 us
    pallas_call x1, Pallas kernels, on_device(): pl.pallas_call(functools.partial(predict_kernel, total_stars), out_shape=...  1.42 us
    broadcast_in_dim x1, local copies, waits for them, and re-layouts, on_device(): return output[None, None]  0.58 us
  transfers between devices with their start and end apart: 7, of which 4 were waited for; matrix products, arithmetic and copies ran while one was open for 0% of the time, Pallas kernels for 29%

commit v1 on v0

--- a/solution.py
+++ b/solution.py
@@ -15,6 +15,7 @@
 SHARERS = 4
 SENT = 7
 LEAN = 4
+PAIR = 2
 
 
 def predict_chunk(pos, vel, acc, jerk, mass, delta, chunk, total_stars):
@@ -70,15 +71,15 @@
 
 def gather(lists, full, splat):
     slots = lists.shape[1]
-    width = SHARERS * slots
+    width = PAIR * slots
     lane = lax.broadcasted_iota(jnp.int32, (8, width), 1)
     whole, base = None, 0
-    for i in range(SHARERS):
+    for i in range(PAIR):
         index = jnp.broadcast_to(lists[2 * i : 2 * i + 1, :], (8, slots))
-        wide = jnp.concatenate([index] * SHARERS, 1)
+        wide = jnp.concatenate([index] * PAIR, 1)
         whole = jnp.where(lane >= base, pltpu.roll(wide, base, 1), whole) if i else wide
         base = base + lists[2 * i + 1, 0]
-    for block in range(SHARERS):
+    for block in range(PAIR):
 
         @pl.when(base > block * slots)
         def _():
@@ -105,15 +106,13 @@
                         )
 
 
-def group_bounds(lists):
-    counts = [lists[2 * owner + 1, 0] for owner in range(SHARERS)]
-    there, here = counts[0] + counts[1], counts[2] + counts[3]
-    return (jnp.maximum(there, here) + 7) // 8, (there + here + 7) // 8
+def group_count(lists):
+    return (lists[1, 0] + lists[3, 0] + 7) // 8
 
 
 def add_lanes(begin, end, sums, flat):
-    slots = flat.shape[1] // SHARERS
-    for block in range(SHARERS):
+    slots = flat.shape[1] // PAIR
+    for block in range(PAIR):
 
         @pl.when((end * 8 > block * slots) & (begin * 8 < (block + 1) * slots))
         def _():
@@ -158,7 +157,7 @@
 
 def near_kernel(lists, full, splat, sums):
     gather(lists, full, splat)
-    _, groups = group_bounds(lists)
+    groups = group_count(lists)
     size = full.shape[0] // (8 * SHARERS)
     place = lax.rem(lax.axis_index("group"), SHARERS)
     odd = lax.rem(place, 2)
@@ -169,28 +168,32 @@
 
 
 def there_kernel(*refs):
-    lists, splat, sums = refs[:3]
-    parts, (blocks, flat, stars, held) = refs[3:-4], refs[-4:]
+    others, lists, splat, sums, own_splat, own_sums = refs[:6]
+    parts, (blocks, flat, stars, held, own_held, wide) = refs[6:-6], refs[-6:]
     begin = 0
     for part in parts:
         stars[pl.ds(begin, part.shape[0]), :] = part[...]
         begin += part.shape[0]
-    shared, _ = group_bounds(lists)
     far = (0, stars.shape[0] // SENT)
-    add_forces(0, shared, splat, stars, far, SENT, 48, sums, held)
-    add_lanes(0, shared, held, flat)
-    for owner in range(2):
-        blocks[owner * 8 : owner * 8 + 8, :] = cut(lists, owner, flat[...], blocks.shape[1])
-
-
-def here_kernel(lists, splat, sums, stars, flat, mine, other, held, rest):
-    shared, groups = group_bounds(lists)
+    there = group_count(others)
+    shared = jnp.maximum(group_count(lists) - there, 0)
+    add_forces(0, there, splat, stars, far, SENT, 48, sums, held)
+    add_forces(0, shared, own_splat, stars, far, SENT, 48, own_sums, own_held)
+    add_lanes(0, there, held, wide)
+    add_lanes(0, shared, own_held, flat)
+    for owner in range(PAIR):
+        blocks[owner * 8 : owner * 8 + 8, :] = cut(others, owner, wide[...], blocks.shape[1])
+
+
+def here_kernel(others, lists, splat, sums, stars, flat, mine, other, held, rest):
+    groups = group_count(lists)
+    shared = jnp.maximum(groups - group_count(others), 0)
     far = (0, stars.shape[0] // SENT)
     add_forces(shared, groups, splat, stars, far, SENT, 48, sums, held)
     add_lanes(shared, groups, held, rest)
     done = lax.broadcasted_iota(jnp.int32, flat.shape, 1) < shared * 8
     whole = jnp.where(done, flat[...], rest[...])
-    for owner, out in ((2, mine), (3, other)):
+    for owner, out in enumerate((mine, other)):
         out[...] = cut(lists, owner, whole, out.shape[1])
 
 
@@ -203,7 +206,7 @@
     total_stars = shard * n_blk
     slots = active_list.shape[2]
     chunks = shard // LANES
-    room = SHARERS * slots
+    room = PAIR * slots
     vmem = pl.BlockSpec(memory_space=pltpu.VMEM)
     smem = pl.BlockSpec(memory_space=pltpu.SMEM)
     params = pltpu.CompilerParams(vmem_limit_bytes=VMEM_LIMIT)
@@ -251,19 +254,26 @@
         parts.append(trade(half, step))
         parts += [swap(part, "blk", bits) for bits in (step + 3, step) if bits]
     core, *others = (swap(packed, "group", bits) for bits in range(1, SHARERS))
-    lists = jnp.concatenate([x[:2] for x in (*others, packed, core)], 0)
-    splat, sums = pl.pallas_call(
-        near_kernel,
-        out_shape=(splat_type, sums_type),
-        in_specs=[vmem] * 2,
-        out_specs=(vmem,) * 2,
-        compiler_params=params,
-        name="near_forces",
-    )(lists, full)
+    lists = jnp.concatenate([packed[:2], core[:2]], 0)
+
+    def near(x, name):
+        return pl.pallas_call(
+            near_kernel,
+            out_shape=(splat_type, sums_type),
+            in_specs=[vmem] * 2,
+            out_specs=(vmem,) * 2,
+            compiler_params=params,
+            name=name,
+        )(x, full)
+
+    own_splat, own_sums = near(lists, "near_own")
+    own_sums, others = lax.optimization_barrier((own_sums, others))
+    others = jnp.concatenate([x[:2] for x in others], 0)
+    splat, sums = near(others, "near_other")
     block_type = jax.ShapeDtypeStruct((8, slots), jnp.float32)
     pairs = slots * shard
     cost = pl.CostEstimate(flops=40 * pairs, bytes_accessed=pairs, transcendentals=pairs)
-    flat_type = jax.ShapeDtypeStruct((8, SHARERS * slots), jnp.float32)
+    flat_type = jax.ShapeDtypeStruct((8, PAIR * slots), jnp.float32)
     stars_type = jax.ShapeDtypeStruct((sum(x.shape[0] for x in parts), LANES), jnp.float32)
     there, flat, stars = pl.pallas_call(
         there_kernel,
@@ -272,18 +282,19 @@
             flat_type,
             stars_type,
         ),
-        in_specs=[vmem] * (3 + len(parts)),
+        in_specs=[vmem] * (6 + len(parts)),
         out_specs=(vmem,) * 3,
-        scratch_shapes=[pltpu.VMEM(sums_type.shape, jnp.float32)],
+        scratch_shapes=[pltpu.VMEM(sums_type.shape, jnp.float32)] * 2
+        + [pltpu.VMEM(flat_type.shape, jnp.float32)],
         compiler_params=params,
         cost_estimate=cost,
         name="there_forces",
-    )(lists, splat, sums, *parts)
+    )(others, lists, splat, sums, own_splat, own_sums, *parts)
     returned = swap(there, "group", 2)
     mine, other = pl.pallas_call(
         here_kernel,
         out_shape=(block_type, block_type),
-        in_specs=[vmem] * 5,
+        in_specs=[vmem] * 6,
         out_specs=(vmem,) * 2,
         scratch_shapes=[
             pltpu.VMEM(sums_type.shape, jnp.float32),
@@ -292,7 +303,7 @@
         compiler_params=params,
         cost_estimate=cost,
         name="here_forces",
-    )(lists, splat, sums, stars, flat)
+    )(others, lists, own_splat, own_sums, stars, flat)
     total = mine + returned[:8] + swap(other + returned[8:], "group", 1)
     live = lax.broadcasted_iota(jnp.int32, (1, slots), 1) < packed[1:2]
     output = jnp.where(live, total[:6], 0.0)

time: 23.7 us -> 24.3 us (1.025)
  the two profiles are of different devices: /device:TPU:23 before, /device:TPU:5 now
where the time goes in v1:
time: 24.3 us; the launch traced here: 23.9 us
  Pallas kernels  15.4 us (63%)
  starting transfers between devices  6.09 us (25%)
  waiting for transfers between devices  1.01 us (4%)
  between operations  0.74 us (3%)
  local copies, waits for them, and re-layouts  0.59 us (2%)
    ppermute x6, starting transfers between devices, swap(): lax.ppermute(x, axis, [(i, i ^ bits) for i in range(lax.axis_size(axis))])  5.93 us
    pallas_call x1, Pallas kernels, on_device(): pl.pallas_call(there_kernel, out_shape=(jax.ShapeDtypeStruct((16, slots),...  5.77 us
    pallas_call x2, Pallas kernels, near(): pl.pallas_call(near_kernel, out_shape=(splat_type, sums_type), in_specs=[...  5.52 us
    pallas_call x1, Pallas kernels, on_device(): pl.pallas_call(here_kernel, out_shape=(block_type, block_type), in_specs=...  2.72 us
    pallas_call x1, Pallas kernels, on_device(): pl.pallas_call(functools.partial(predict_kernel, total_stars), out_shape=...  1.42 us
    ppermute x6, waiting for transfers between devices, swap(): lax.ppermute(x, axis, [(i, i ^ bits) for i in range(lax.axis_size(axis))])  1.01 us
    broadcast_in_dim x1, local copies, waits for them, and re-layouts, on_device(): return output[None, None]  0.58 us
  transfers between devices with their start and end apart: 7, of which 1 were waited for; matrix products, arithmetic and copies ran while one was open for 0% of the time, Pallas kernels for 34%

profile of v1, /device:TPU:5, one launch (start us, length us, event | category | flops | bytes accessed | tf_op | source)
XLA Modules:
  0.0 23.9 jit_solution(13780769060436471264)
XLA Ops:
  0.7 1.4 %predict.1 = (f32[512,128]{1,0:T(8,128)S(1)}, f32[112,128]{1,0:T(8,128)S(1)}, f32[224,128]{1,0:T(8,128)S(1)}, s32[8,128]{1,0:T(8,128)S(1)}) custom-call(f32[3,8192]{1,0:T(4,128)} %refs_0_.1, f32[3,8192]{1,0:T(4,128)} %refs_1_.1, f32[3,8192]{1,0:T(4,128)} %refs_2_.1, f32[3,8192]{1,0:T(4,128)} %refs_3_.1, f32[64,128]{1,0:T(8,128)} %bitcast.7, ...), custom_call_target="tpu_custom_call" | custom-call | tf_op jit(solution)/shard_map/predict/pallas_call | solution.py:237
  2.1 0.7 %collective-permute-start = (s32[8,128]{1,0:T(8,128)S(1)}, s32[8,128]{1,0:T(8,128)S(1)}, u32[]{:S(2)}, u32[]{:S(2)}) collective-permute-start(s32[8,128]{1,0:T(8,128)S(1)} %get-tuple-element.21), channel_id=1, source_target_pairs={{0,1},{1,0},{2,3},{3,2},{4,5},{5,4},{6,7},{7,6},{8,9},{9,8},{10,11... | collective-permute-start | bytes 12296 | tf_op jit(solution)/shard_map/ppermute | solution.py:226
  2.8 1.3 %collective-permute-start.2 = (s32[8,128]{1,0:T(8,128)S(1)}, s32[8,128]{1,0:T(8,128)S(1)}, u32[]{:S(2)}, u32[]{:S(2)}) collective-permute-start(s32[8,128]{1,0:T(8,128)S(1)} %get-tuple-element.21), channel_id=1, source_target_pairs={{0,3},{1,2},{2,1},{3,0},{4,7},{5,6},{6,5},{7,4},{8,11},{9,10},{10,... | collective-permute-start | bytes 12296 | tf_op jit(solution)/shard_map/ppermute | solution.py:226
  4.1 0.2 collective-permute-start.1
  4.2 1.2 %collective-permute-start.4 = (f32[112,128]{1,0:T(8,128)S(1)}, f32[112,128]{1,0:T(8,128)S(1)}, u32[]{:S(2)}, u32[]{:S(2)}) collective-permute-start(f32[112,128]{1,0:T(8,128)S(1)} %get-tuple-element.31), channel_id=1, source_target_pairs={{0,24},{8,16},{16,8},{24,0},{1,25},{9,17},{17,9},{25,1},{2,26},{10... | collective-permute-start | bytes 172040 | tf_op jit(solution)/shard_map/ppermute | solution.py:226
  5.4 0.2 collective-permute-start.3
  5.6 0.0 collective-permute-done
  5.6 3.9 %near_own.1 = (f32[2048,128]{1,0:T(8,128)S(1)}, f32[6,256,128]{2,1,0:T(8,128)S(1)}) custom-call(s32[4,128]{1,0:T(4,128)S(1)} %pad_add_fusion.lists.refs_1_, f32[512,128]{1,0:T(8,128)S(1)} %get-tuple-element.22.full), custom_call_target="tpu_custom_call" | custom-call | tf_op jit(solution)/shard_map/near_own/pallas_call | solution.py:260
  9.4 0.0 collective-permute-done.2
  9.4 0.0 collective-permute-done.1
  9.5 1.7 %near_other.1 = (f32[2048,128]{1,0:T(8,128)S(1)}, f32[6,256,128]{2,1,0:T(8,128)S(1)}) custom-call(s32[4,128]{1,0:T(4,128)S(1)} %pad_add_fusion.1.lists.refs_0_.others, f32[512,128]{1,0:T(8,128)S(1)} %get-tuple-element.22.full), custom_call_target="tpu_custom_call" | custom-call | tf_op jit(solution)/shard_map/near_other/pallas_call | solution.py:260
  11.2 0.0 collective-permute-done.4.refs_7_
  11.2 0.0 collective-permute-done.3.refs_6_
  11.2 5.8 %there_forces.1 = (f32[16,128]{1,0:T(8,128)S(1)}, f32[8,256]{1,0:T(8,128)S(1)}, f32[336,128]{1,0:T(8,128)S(1)}) custom-call(s32[4,128]{1,0:T(4,128)S(1)} %pad_add_fusion.1.lists.refs_0_.others, s32[4,128]{1,0:T(4,128)S(1)} %pad_add_fusion.lists.refs_1_, f32[2048,128]{1,0:T(8,128)S(1)} %get-tuple-element.28.refs_2_, ...), custom_call_target="tpu_custom_call" | custom-call | flops 41943040 | bytes 1048576 | tf_op jit(solution)/shard_map/there_forces/pallas_call | solution.py:278
  17.0 2.4 %collective-permute-start.5 = (f32[16,128]{1,0:T(8,128)S(1)}, f32[16,128]{1,0:T(8,128)S(1)}, u32[]{:S(2)}, u32[]{:S(2)}) collective-permute-start(f32[16,128]{1,0:T(8,128)S(1)} %get-tuple-element.35), channel_id=1, source_target_pairs={{0,2},{1,3},{2,0},{3,1},{4,6},{5,7},{6,4},{7,5},{8,10},{9,11},{10,... | collective-permute-start | bytes 24584 | tf_op jit(solution)/shard_map/ppermute | solution.py:226
  19.4 2.7 %here_forces.1 = (f32[8,128]{1,0:T(8,128)S(1)}, f32[8,128]{1,0:T(8,128)S(1)}) custom-call(s32[4,128]{1,0:T(4,128)S(1)} %pad_add_fusion.1.lists.refs_0_.others, s32[4,128]{1,0:T(4,128)S(1)} %pad_add_fusion.lists.refs_1_, f32[2048,128]{1,0:T(8,128)S(1)} %get-tuple-element.26.refs_4_.splat, f32[6,256,128]{2,1,0:T(8,128)S(1)} %get-tuple-element.27.refs_5_.sums, ...), custom_call_target="tpu_custom_call" | custom-call | flops 41943040 | bytes 1048576 | tf_op jit(solution)/shard_map/here_forces/pallas_call | solution.py:294
  22.1 0.0 collective-permute-done.5
  22.1 0.2 collective-permute-start.6
  22.3 1.0 %collective-permute-done.6 = f32[8,128]{1,0:T(8,128)S(1)} collective-permute-done((f32[8,128]{1,0:T(8,128)S(1)}, f32[8,128]{1,0:T(8,128)S(1)}, u32[]{:S(2)}, u32[]{:S(2)}) %collective-permute-start.6) | collective-permute-done | bytes 4128 | tf_op jit(solution)/shard_map/ppermute | solution.py:226
  23.3 0.6 %copy.9 = f32[1,1,6,128]{3,1,2,0:T(1,128)} copy(f32[1,1,6,128]{3,2,1,0:T(8,128)S(1)} %select_bitcast_fusion) | data formatting | bytes 6144 | tf_op jit(solution)/shard_map/broadcast_in_dim | solution.py:310
  (10 shorter events, 0.0 us)
Async XLA Ops:
  2.1 3.5 %collective-permute-start = (s32[8,128]{1,0:T(8,128)S(1)}, s32[8,128]{1,0:T(8,128)S(1)}, u32[]{:S(2)}, u32[]{:S(2)}) collective-permute-start(s32[8,128]{1,0:T(8,128)S(1)} %get-tuple-element.21), channel_id=1, source_target_pairs={{0,1},{1,0},{2,3},{3,2},{4,5},{5,4},{6,7},{7,6},{8,9},{9,8},{10,11... | collective-permute-start | bytes 12296 | tf_op jit(solution)/shard_map/ppermute | solution.py:226
  2.8 6.6 %collective-permute-start.2 = (s32[8,128]{1,0:T(8,128)S(1)}, s32[8,128]{1,0:T(8,128)S(1)}, u32[]{:S(2)}, u32[]{:S(2)}) collective-permute-start(s32[8,128]{1,0:T(8,128)S(1)} %get-tuple-element.21), channel_id=1, source_target_pairs={{0,3},{1,2},{2,1},{3,0},{4,7},{5,6},{6,5},{7,4},{8,11},{9,10},{10,... | collective-permute-start | bytes 12296 | tf_op jit(solution)/shard_map/ppermute | solution.py:226
  4.1 5.4 %collective-permute-start.1 = (s32[8,128]{1,0:T(8,128)S(1)}, s32[8,128]{1,0:T(8,128)S(1)}, u32[]{:S(2)}, u32[]{:S(2)}) collective-permute-start(s32[8,128]{1,0:T(8,128)S(1)} %get-tuple-element.21), channel_id=1, source_target_pairs={{0,2},{1,3},{2,0},{3,1},{4,6},{5,7},{6,4},{7,5},{8,10},{9,11},{10,... | collective-permute-start | bytes 12296 | tf_op jit(solution)/shard_map/ppermute | solution.py:226
  4.2 6.9 %collective-permute-start.4 = (f32[112,128]{1,0:T(8,128)S(1)}, f32[112,128]{1,0:T(8,128)S(1)}, u32[]{:S(2)}, u32[]{:S(2)}) collective-permute-start(f32[112,128]{1,0:T(8,128)S(1)} %get-tuple-element.31), channel_id=1, source_target_pairs={{0,24},{8,16},{16,8},{24,0},{1,25},{9,17},{17,9},{25,1},{2,26},{10... | collective-permute-start | bytes 172040 | tf_op jit(solution)/shard_map/ppermute | solution.py:226
  5.4 5.8 %collective-permute-start.3 = (f32[224,128]{1,0:T(8,128)S(1)}, f32[224,128]{1,0:T(8,128)S(1)}, u32[]{:S(2)}, u32[]{:S(2)}) collective-permute-start(f32[224,128]{1,0:T(8,128)S(1)} %get-tuple-element.30), channel_id=1, source_target_pairs={{0,8},{1,9},{2,18},{3,19},{4,12},{5,13},{6,22},{7,23},{8,0},{9,1},... | collective-permute-start | bytes 344072 | tf_op jit(solution)/shard_map/ppermute | solution.py:234
  17.0 5.1 %collective-permute-start.5 = (f32[16,128]{1,0:T(8,128)S(1)}, f32[16,128]{1,0:T(8,128)S(1)}, u32[]{:S(2)}, u32[]{:S(2)}) collective-permute-start(f32[16,128]{1,0:T(8,128)S(1)} %get-tuple-element.35), channel_id=1, source_target_pairs={{0,2},{1,3},{2,0},{3,1},{4,6},{5,7},{6,4},{7,5},{8,10},{9,11},{10,... | collective-permute-start | bytes 24584 | tf_op jit(solution)/shard_map/ppermute | solution.py:226
  22.1 1.2 %collective-permute-start.6 = (f32[8,128]{1,0:T(8,128)S(1)}, f32[8,128]{1,0:T(8,128)S(1)}, u32[]{:S(2)}, u32[]{:S(2)}) collective-permute-start(f32[8,128]{1,0:T(8,128)S(1)} %slice_add_fusion), channel_id=1, source_target_pairs={{0,1},{1,0},{2,3},{3,2},{4,5},{5,4},{6,7},{7,6},{8,9},{9,8},{10,11... | collective-permute-start | bytes 12296 | tf_op jit(solution)/shard_map/ppermute | solution.py:226

commit v2 on v0

--- a/solution.py
+++ b/solution.py
@@ -14,7 +14,7 @@
 SPREAD = 32
 SHARERS = 4
 SENT = 7
-LEAN = 4
+LEAN = 6
 
 
 def predict_chunk(pos, vel, acc, jerk, mass, delta, chunk, total_stars):

time: 23.7 us -> 23.9 us (level)
  the two profiles are of different devices: /device:TPU:23 before, /device:TPU:0 now
where the time goes in v2:
time: 23.9 us; the launch traced here: 23.7 us
  Pallas kernels  11.2 us (47%)
  starting transfers between devices  7.81 us (33%)
  waiting for transfers between devices  3.39 us (14%)
  between operations  0.69 us (3%)
  local copies, waits for them, and re-layouts  0.59 us (2%)
    ppermute x6, starting transfers between devices, swap(): lax.ppermute(x, axis, [(i, i ^ bits) for i in range(lax.axis_size(axis))])  5.91 us
    pallas_call x1, Pallas kernels, on_device(): pl.pallas_call(there_kernel, out_shape=(jax.ShapeDtypeStruct((16, slots),...  5.51 us
    ppermute x6, waiting for transfers between devices, swap(): lax.ppermute(x, axis, [(i, i ^ bits) for i in range(lax.axis_size(axis))])  3.38 us
    pallas_call x1, Pallas kernels, on_device(): pl.pallas_call(near_kernel, out_shape=(splat_type, sums_type), in_specs=[...  2.81 us
    ppermute x1, starting transfers between devices, trade(): return lax.ppermute(x, ('blk', 'group'), pairs)  1.9 us
    pallas_call x1, Pallas kernels, on_device(): pl.pallas_call(here_kernel, out_shape=(block_type, block_type), in_specs=...  1.45 us
    pallas_call x1, Pallas kernels, on_device(): pl.pallas_call(functools.partial(predict_kernel, total_stars), out_shape=...  1.42 us
    broadcast_in_dim x1, local copies, waits for them, and re-layouts, on_device(): return output[None, None]  0.58 us
  transfers between devices with their start and end apart: 7, of which 4 were waited for; matrix products, arithmetic and copies ran while one was open for 0% of the time, Pallas kernels for 18%

profile of v2, /device:TPU:0, one launch (start us, length us, event | category | flops | bytes accessed | tf_op | source)
XLA Modules:
  0.0 23.7 jit_solution(16933227406041474909)
XLA Ops:
  0.7 1.4 %predict.1 = (f32[512,128]{1,0:T(8,128)S(1)}, f32[112,128]{1,0:T(8,128)S(1)}, f32[224,128]{1,0:T(8,128)S(1)}, s32[8,128]{1,0:T(8,128)S(1)}) custom-call(f32[3,8192]{1,0:T(4,128)} %refs_0_.1, f32[3,8192]{1,0:T(4,128)} %refs_1_.1, f32[3,8192]{1,0:T(4,128)} %refs_2_.1, f32[3,8192]{1,0:T(4,128)} %refs_3_.1, f32[64,128]{1,0:T(8,128)} %bitcast.7, ...), custom_call_target="tpu_custom_call" | custom-call | tf_op jit(solution)/shard_map/predict/pallas_call | solution.py:234
  2.1 0.5 %collective-permute-start.2 = (s32[8,128]{1,0:T(8,128)S(1)}, s32[8,128]{1,0:T(8,128)S(1)}, u32[]{:S(2)}, u32[]{:S(2)}) collective-permute-start(s32[8,128]{1,0:T(8,128)S(1)} %get-tuple-element.16), channel_id=1, source_target_pairs={{0,1},{1,0},{2,3},{3,2},{4,5},{5,4},{6,7},{7,6},{8,9},{9,8},{10,11... | collective-permute-start | bytes 12296 | tf_op jit(solution)/shard_map/ppermute | solution.py:223
  2.6 2.7 %collective-permute-start.1 = (s32[8,128]{1,0:T(8,128)S(1)}, s32[8,128]{1,0:T(8,128)S(1)}, u32[]{:S(2)}, u32[]{:S(2)}) collective-permute-start(s32[8,128]{1,0:T(8,128)S(1)} %get-tuple-element.16), channel_id=1, source_target_pairs={{0,3},{1,2},{2,1},{3,0},{4,7},{5,6},{6,5},{7,4},{8,11},{9,10},{10,... | collective-permute-start | bytes 12296 | tf_op jit(solution)/shard_map/ppermute | solution.py:223
  5.3 0.0 collective-permute-start
  5.3 1.9 %collective-permute-start.3 = (f32[224,128]{1,0:T(8,128)S(1)}, f32[224,128]{1,0:T(8,128)S(1)}, u32[]{:S(2)}, u32[]{:S(2)}) collective-permute-start(f32[224,128]{1,0:T(8,128)S(1)} %get-tuple-element.20), channel_id=1, source_target_pairs={{0,8},{1,9},{2,18},{3,19},{4,12},{5,13},{6,22},{7,23},{8,0},{9,1},... | collective-permute-start | bytes 344072 | tf_op jit(solution)/shard_map/ppermute | solution.py:231
  7.2 1.5 %collective-permute-start.4 = (f32[112,128]{1,0:T(8,128)S(1)}, f32[112,128]{1,0:T(8,128)S(1)}, u32[]{:S(2)}, u32[]{:S(2)}) collective-permute-start(f32[112,128]{1,0:T(8,128)S(1)} %get-tuple-element.21), channel_id=1, source_target_pairs={{0,24},{8,16},{16,8},{24,0},{1,25},{9,17},{17,9},{25,1},{2,26},{10... | collective-permute-start | bytes 172040 | tf_op jit(solution)/shard_map/ppermute | solution.py:223
  8.7 0.0 collective-permute-done.2
  8.7 0.0 collective-permute-done.1
  8.8 0.2 collective-permute-done
  8.9 2.8 %near_forces.1 = (f32[4096,128]{1,0:T(8,128)S(1)}, f32[6,512,128]{2,1,0:T(8,128)S(1)}) custom-call(s32[8,128]{1,0:T(8,128)S(1)} %pad_add_fusion.lists.refs_0_, f32[512,128]{1,0:T(8,128)S(1)} %get-tuple-element.17.full), custom_call_target="tpu_custom_call" | custom-call | tf_op jit(solution)/shard_map/near_forces/pallas_call | solution.py:255
  11.7 1.0 %collective-permute-done.4.refs_4_ = f32[112,128]{1,0:T(8,128)S(1)} collective-permute-done((f32[112,128]{1,0:T(8,128)S(1)}, f32[112,128]{1,0:T(8,128)S(1)}, u32[]{:S(2)}, u32[]{:S(2)}) %collective-permute-start.4) | collective-permute-done | bytes 57376 | tf_op jit(solution)/shard_map/ppermute | solution.py:223
  12.8 0.0 collective-permute-done.3.refs_3_
  12.8 5.5 %there_forces.1 = (f32[16,128]{1,0:T(8,128)S(1)}, f32[8,512]{1,0:T(8,128)S(1)}, f32[336,128]{1,0:T(8,128)S(1)}) custom-call(s32[8,128]{1,0:T(8,128)S(1)} %pad_add_fusion.lists.refs_0_, f32[4096,128]{1,0:T(8,128)S(1)} %get-tuple-element.18.refs_1_.splat, f32[6,512,128]{2,1,0:T(8,128)S(1)} %get-tuple-element.19.refs_2_.sums, ...), custom_call_target="tpu_custom_call" | custom-call | flops 41943040 | bytes 1048576 | tf_op jit(solution)/shard_map/there_forces/pallas_call | solution.py:268
  18.3 1.2 %collective-permute-start.5 = (f32[16,128]{1,0:T(8,128)S(1)}, f32[16,128]{1,0:T(8,128)S(1)}, u32[]{:S(2)}, u32[]{:S(2)}) collective-permute-start(f32[16,128]{1,0:T(8,128)S(1)} %get-tuple-element.25), channel_id=1, source_target_pairs={{0,2},{1,3},{2,0},{3,1},{4,6},{5,7},{6,4},{7,5},{8,10},{9,11},{10,... | collective-permute-start | bytes 24584 | tf_op jit(solution)/shard_map/ppermute | solution.py:223
  19.4 1.4 %here_forces.1 = (f32[8,128]{1,0:T(8,128)S(1)}, f32[8,128]{1,0:T(8,128)S(1)}) custom-call(s32[8,128]{1,0:T(8,128)S(1)} %pad_add_fusion.lists.refs_0_, f32[4096,128]{1,0:T(8,128)S(1)} %get-tuple-element.18.refs_1_.splat, f32[6,512,128]{2,1,0:T(8,128)S(1)} %get-tuple-element.19.refs_2_.sums, f32[336,128]{1,0:T(8,128)S(1)} %get-tuple-element.22.stars, ...), custom_call_target="tpu_custom_call" | custom-call | flops 41943040 | bytes 1048576 | tf_op jit(solution)/shard_map/here_forces/pallas_call | solution.py:283
  20.9 1.0 %collective-permute-done.5 = f32[16,128]{1,0:T(8,128)S(1)} collective-permute-done((f32[16,128]{1,0:T(8,128)S(1)}, f32[16,128]{1,0:T(8,128)S(1)}, u32[]{:S(2)}, u32[]{:S(2)}) %collective-permute-start.5) | collective-permute-done | bytes 8224 | tf_op jit(solution)/shard_map/ppermute | solution.py:223
  21.9 0.0 collective-permute-start.6
  22.0 1.2 %collective-permute-done.6 = f32[8,128]{1,0:T(8,128)S(1)} collective-permute-done((f32[8,128]{1,0:T(8,128)S(1)}, f32[8,128]{1,0:T(8,128)S(1)}, u32[]{:S(2)}, u32[]{:S(2)}) %collective-permute-start.6) | collective-permute-done | bytes 4128 | tf_op jit(solution)/shard_map/ppermute | solution.py:223
  23.1 0.6 %copy.9 = f32[1,1,6,128]{3,1,2,0:T(1,128)} copy(f32[1,1,6,128]{3,2,1,0:T(8,128)S(1)} %select_bitcast_fusion) | data formatting | bytes 6144 | tf_op jit(solution)/shard_map/broadcast_in_dim | solution.py:299
  (9 shorter events, 0.0 us)
Async XLA Ops:
  2.1 6.7 %collective-permute-start.2 = (s32[8,128]{1,0:T(8,128)S(1)}, s32[8,128]{1,0:T(8,128)S(1)}, u32[]{:S(2)}, u32[]{:S(2)}) collective-permute-start(s32[8,128]{1,0:T(8,128)S(1)} %get-tuple-element.16), channel_id=1, source_target_pairs={{0,1},{1,0},{2,3},{3,2},{4,5},{5,4},{6,7},{7,6},{8,9},{9,8},{10,11... | collective-permute-start | bytes 12296 | tf_op jit(solution)/shard_map/ppermute | solution.py:223
  2.6 6.1 %collective-permute-start.1 = (s32[8,128]{1,0:T(8,128)S(1)}, s32[8,128]{1,0:T(8,128)S(1)}, u32[]{:S(2)}, u32[]{:S(2)}) collective-permute-start(s32[8,128]{1,0:T(8,128)S(1)} %get-tuple-element.16), channel_id=1, source_target_pairs={{0,3},{1,2},{2,1},{3,0},{4,7},{5,6},{6,5},{7,4},{8,11},{9,10},{10,... | collective-permute-start | bytes 12296 | tf_op jit(solution)/shard_map/ppermute | solution.py:223
  5.3 3.6 %collective-permute-start = (s32[8,128]{1,0:T(8,128)S(1)}, s32[8,128]{1,0:T(8,128)S(1)}, u32[]{:S(2)}, u32[]{:S(2)}) collective-permute-start(s32[8,128]{1,0:T(8,128)S(1)} %get-tuple-element.16), channel_id=1, source_target_pairs={{0,2},{1,3},{2,0},{3,1},{4,6},{5,7},{6,4},{7,5},{8,10},{9,11},{10,... | collective-permute-start | bytes 12296 | tf_op jit(solution)/shard_map/ppermute | solution.py:223
  5.3 7.4 %collective-permute-start.3 = (f32[224,128]{1,0:T(8,128)S(1)}, f32[224,128]{1,0:T(8,128)S(1)}, u32[]{:S(2)}, u32[]{:S(2)}) collective-permute-start(f32[224,128]{1,0:T(8,128)S(1)} %get-tuple-element.20), channel_id=1, source_target_pairs={{0,8},{1,9},{2,18},{3,19},{4,12},{5,13},{6,22},{7,23},{8,0},{9,1},... | collective-permute-start | bytes 344072 | tf_op jit(solution)/shard_map/ppermute | solution.py:231
  7.2 5.5 %collective-permute-start.4 = (f32[112,128]{1,0:T(8,128)S(1)}, f32[112,128]{1,0:T(8,128)S(1)}, u32[]{:S(2)}, u32[]{:S(2)}) collective-permute-start(f32[112,128]{1,0:T(8,128)S(1)} %get-tuple-element.21), channel_id=1, source_target_pairs={{0,24},{8,16},{16,8},{24,0},{1,25},{9,17},{17,9},{25,1},{2,26},{10... | collective-permute-start | bytes 172040 | tf_op jit(solution)/shard_map/ppermute | solution.py:223
  18.3 3.7 %collective-permute-start.5 = (f32[16,128]{1,0:T(8,128)S(1)}, f32[16,128]{1,0:T(8,128)S(1)}, u32[]{:S(2)}, u32[]{:S(2)}) collective-permute-start(f32[16,128]{1,0:T(8,128)S(1)} %get-tuple-element.25), channel_id=1, source_target_pairs={{0,2},{1,3},{2,0},{3,1},{4,6},{5,7},{6,4},{7,5},{8,10},{9,11},{10,... | collective-permute-start | bytes 24584 | tf_op jit(solution)/shard_map/ppermute | solution.py:223
  21.9 1.2 %collective-permute-start.6 = (f32[8,128]{1,0:T(8,128)S(1)}, f32[8,128]{1,0:T(8,128)S(1)}, u32[]{:S(2)}, u32[]{:S(2)}) collective-permute-start(f32[8,128]{1,0:T(8,128)S(1)} %slice_add_fusion), channel_id=1, source_target_pairs={{0,1},{1,0},{2,3},{3,2},{4,5},{5,4},{6,7},{7,6},{8,9},{9,8},{10,11... | collective-permute-start | bytes 12296 | tf_op jit(solution)/shard_map/ppermute | solution.py:223
